TPU v7x, 32 devices: a whole 2x2x4 slice. The times are simulated.
32 devices in a mesh: section: 4 (over y, core), ctx: 4 (over z), dp: 2 (over x).
Axes of the slice: x: 2, y: 2, z: 4, core: 2. Of those that a mesh axis runs over, the one named last changes fastest.
Arguments:
- q_in: bfloat16 [2, 4, 512, 2048], P('dp', 'section', 'ctx'), may hold values from -6 to 6
- key_input: bfloat16 [2, 4, 512, 512], P('dp', 'section', 'ctx'), may hold values from -6 to 6
- value_input: bfloat16 [2, 4, 512, 512], P('dp', 'section', 'ctx'), may hold values from -6 to 6
- output_saved: bfloat16 [2, 4, 512, 2048], P('dp', 'section', 'ctx'), may hold values from -6 to 6
- output_gradient: bfloat16 [2, 4, 512, 2048], P('dp', 'section', 'ctx'), may hold values from -6 to 6
- lse: float32 [2, 4, 16, 512], P('dp', 'section', None, 'ctx'), may hold values from 2 to 5
- bias_q: bfloat16 [4, 2048], P('section'), may hold values from -3 to 3
- key_bias: bfloat16 [4, 512], P('section'), may hold values from -3 to 3
- value_bias: bfloat16 [4, 512], P('section'), may hold values from -3 to 3
Outputs:
- recv_q: bfloat16 [2, 4, 512, 2048], P('dp', 'section', 'ctx')
- recv_k: bfloat16 [2, 4, 512, 512], P('dp', 'section', 'ctx')
- recv_v: bfloat16 [2, 4, 512, 512], P('dp', 'section', 'ctx')
- grad_bq: float32 [4, 2048], P('section')
- grad_bk: float32 [4, 512], P('section')
- grad_bv: float32 [4, 512], P('section')
All inputs are finite; a program needn't handle non-finite values.
Results may differ from a plain program's by a relative error of at most 0.0035.
The roundings to bfloat16 on the way count: a program that leaves them out, or rounds other values in their place, can miss the bound.
Values may be sent and summed in bfloat16 or wider, within the bound.
A program may use at most 64 MiB of HBM per device.

v0:
```python
import math

import jax
import jax.numpy as jnp
from jax import lax
from jax.sharding import PartitionSpec as P

QUERY_HEADS = 16
KEY_VALUE_HEADS = 4
HEAD_SIZE = 128


def passed_along(value, axis, by):
    size = lax.axis_size(axis)
    return lax.ppermute(value, axis, [(i, (i + by) % size) for i in range(size)])


def shifted(value, axis, by):
    size = lax.axis_size(axis)
    pairs = [(i, i + by) for i in range(size) if 0 <= i + by < size]
    return lax.ppermute(value, axis, pairs)


def token_position(rows, block_rows, block_count):
    half_rows = block_rows // 2
    owner = rows // block_rows
    local = rows % block_rows
    early = owner * half_rows + local
    late = (2 * block_count - 1 - owner) * half_rows + local - half_rows
    return jnp.where(local < half_rows, early, late)


def block_terms(
    query_grouped,
    output_gradient_grouped,
    row_delta,
    logsumexp_grouped,
    q_pos,
    key_value_piece,
    k_pos,
):
    piece_row_count = key_value_piece.shape[0]
    token_rows = query_grouped.shape[0]
    key_value_width = KEY_VALUE_HEADS * HEAD_SIZE
    att_scale = 1.0 / math.sqrt(HEAD_SIZE)
    key_row_list = key_value_piece[:, :key_value_width].reshape(
        piece_row_count, KEY_VALUE_HEADS, HEAD_SIZE
    )
    value_row_list = key_value_piece[:, key_value_width:].reshape(
        piece_row_count, KEY_VALUE_HEADS, HEAD_SIZE
    )
    scores = (
        jnp.einsum(
            "ikgd,jkd->kgij", query_grouped, key_row_list, preferred_element_type=jnp.float32
        )
        * att_scale
    )
    causal = k_pos[None, :] <= q_pos[:, None]
    soft_prob = jnp.where(causal, jnp.exp(scores - logsumexp_grouped[..., None]), 0.0)
    grad_prob = jnp.einsum(
        "ikgd,jkd->kgij",
        output_gradient_grouped,
        value_row_list,
        preferred_element_type=jnp.float32,
    )
    grad_score = soft_prob * (grad_prob - row_delta[..., None])
    prob_low = soft_prob.astype(jnp.bfloat16)
    score_low = grad_score.astype(jnp.bfloat16)
    grad_q = (
        jnp.einsum("kgij,jkd->ikgd", score_low, key_row_list, preferred_element_type=jnp.float32)
        * att_scale
    )
    key_gradient = (
        jnp.einsum("kgij,ikgd->jkd", score_low, query_grouped, preferred_element_type=jnp.float32)
        * att_scale
    )
    value_gradient = jnp.einsum(
        "kgij,ikgd->jkd", prob_low, output_gradient_grouped, preferred_element_type=jnp.float32
    )
    kv_terms = jnp.concatenate(
        [
            key_gradient.reshape(piece_row_count, key_value_width),
            value_gradient.reshape(piece_row_count, key_value_width),
        ],
        axis=1,
    )
    return (grad_q.reshape(token_rows, QUERY_HEADS * HEAD_SIZE), kv_terms)


def body(
    q_in, key_input, value_input, output_saved, output_gradient, lse, bias_q, key_bias, value_bias
):
    token_rows = q_in.shape[2]
    query_groups = QUERY_HEADS // KEY_VALUE_HEADS
    width_q = QUERY_HEADS * HEAD_SIZE
    key_value_width = KEY_VALUE_HEADS * HEAD_SIZE
    ctx_count = lax.axis_size("ctx")
    ctx_index = lax.axis_index("ctx")
    query_lowered = (q_in[0, 0].astype(jnp.float32) + bias_q.astype(jnp.float32)).astype(
        jnp.bfloat16
    )
    key_lowered = (key_input[0, 0].astype(jnp.float32) + key_bias.astype(jnp.float32)).astype(
        jnp.bfloat16
    )
    value_lowered = (value_input[0, 0].astype(jnp.float32) + value_bias.astype(jnp.float32)).astype(
        jnp.bfloat16
    )
    kv_own = jnp.concatenate([key_lowered, value_lowered], axis=1)
    query_grouped = query_lowered.reshape(token_rows, KEY_VALUE_HEADS, query_groups, HEAD_SIZE)
    output_gradient_grouped = output_gradient[0, 0].reshape(
        token_rows, KEY_VALUE_HEADS, query_groups, HEAD_SIZE
    )
    output_grouped = output_saved[0, 0].reshape(
        token_rows, KEY_VALUE_HEADS, query_groups, HEAD_SIZE
    )
    row_delta = jnp.transpose(
        jnp.sum(
            output_gradient_grouped.astype(jnp.float32) * output_grouped.astype(jnp.float32),
            axis=-1,
        ),
        (1, 2, 0),
    )
    logsumexp_grouped = lse[0, 0].reshape(KEY_VALUE_HEADS, query_groups, token_rows)
    local_rows = jnp.arange(token_rows, dtype=jnp.int32)
    q_pos = token_position(ctx_index * token_rows + local_rows, token_rows, ctx_count)
    grad_q = jnp.zeros((token_rows, width_q), jnp.float32)
    kv_block = kv_own
    kv_grads = jnp.zeros((token_rows, 2 * key_value_width), jnp.float32)
    for cycle_step in range(ctx_count):
        kv_owner = (ctx_index + cycle_step) % ctx_count
        k_pos = token_position(kv_owner * token_rows + local_rows, token_rows, ctx_count)
        q_term, kv_terms = block_terms(
            query_grouped,
            output_gradient_grouped,
            row_delta,
            logsumexp_grouped,
            q_pos,
            kv_block,
            k_pos,
        )
        grad_q = grad_q + q_term
        kv_grads = kv_grads + kv_terms
        if cycle_step + 1 < ctx_count:
            kv_block = passed_along(kv_block, "ctx", -1)
        kv_grads = passed_along(kv_grads, "ctx", -1)
    sum_q, sum_k, sum_v = lax.psum(
        (
            jnp.sum(grad_q, axis=0, keepdims=True),
            jnp.sum(kv_grads[:, :key_value_width], axis=0, keepdims=True),
            jnp.sum(kv_grads[:, key_value_width:], axis=0, keepdims=True),
        ),
        ("ctx", "dp"),
    )
    outgoing = jnp.concatenate([grad_q.astype(jnp.bfloat16), kv_grads.astype(jnp.bfloat16)], axis=1)
    incoming = shifted(outgoing, "section", -1)
    recv_q = incoming[:, :width_q][None, None]
    recv_k = incoming[:, width_q : width_q + key_value_width][None, None]
    recv_v = incoming[:, width_q + key_value_width :][None, None]
    return (recv_q, recv_k, recv_v, sum_q, sum_k, sum_v)


def solution(mesh):
    return jax.shard_map(
        body,
        mesh=mesh,
        in_specs=(
            P("dp", "section", "ctx", None),
            P("dp", "section", "ctx", None),
            P("dp", "section", "ctx", None),
            P("dp", "section", "ctx", None),
            P("dp", "section", "ctx", None),
            P("dp", "section", None, "ctx"),
            P("section", None),
            P("section", None),
            P("section", None),
        ),
        out_specs=(
            P("dp", "section", "ctx", None),
            P("dp", "section", "ctx", None),
            P("dp", "section", "ctx", None),
            P("section", None),
            P("section", None),
            P("section", None),
        ),
        check_vma=False,
    )
```

profile of v0, /device:TPU:0, one launch (start us, length us, event | category | flops | bytes accessed | tf_op | source)
XLA Modules:
  0.0 139.5 jit_solution(1919349859205784991)
XLA Ops:
  0.7 1.5 %reshape_squeeze.4 = bf16[128,4,4,128]{3,2,1,0:T(4,128)(2,1)S(1)} reshape(bf16[1,1,128,2048]{3,2,1,0:T(8,128)(2,1)} %param.13) | data formatting | bytes 1048576 | tf_op jit(solution)/shard_map/reshape;squeeze | solution.py:110
  5.7 2.9 %reshape.308 = f32[128,4,4,128]{3,2,1,0:T(4,128)} reshape(bf16[1,1,128,2048]{3,2,1,0:T(8,128)(2,1)} %param.12) | data formatting | bytes 1572864 | tf_op jit(solution)/shard_map/convert_element_type | solution.py:118
  8.6 2.0 %multiply_reduce_fusion = f32[128,4,4]{2,1,0:T(4,128)S(1)} fusion(f32[128,4,4,128]{3,2,1,0:T(4,128)} %reshape.308, bf16[128,4,4,128]{3,2,1,0:T(4,128)(2,1)S(1)} %reshape_squeeze.4), kind=kLoop, calls=%fused_computation.48 | loop fusion | flops 784384 | bytes 1581056 | tf_op jit(solution)/shard_map/reduce_sum | solution.py:117
  13.2 5.0 %collective-permute-start.3 = (f32[128,1024]{1,0:T(8,128)}, f32[128,1024]{1,0:T(8,128)S(1)}, u32[]{:S(2)}, u32[]{:S(2)}) collective-permute-start(f32[128,1024]{1,0:T(8,128)} %pad_maximum_fusion.1), channel_id=1, source_target_pairs={{0,6},{2,0},{4,2},{6,4},{1,7},{3,1},{5,3},{7,5},{8,14},{10,8},{12,... | collective-permute-start | bytes 1572872 | tf_op jit(solution)/shard_map/ppermute | solution.py:15
  19.4 15.9 %collective-permute-done = bf16[128,1024]{0,1:T(8,128)(2,1)S(1)} collective-permute-done((bf16[128,1024]{0,1:T(8,128)(2,1)S(1)}, bf16[128,1024]{0,1:T(8,128)(2,1)S(1)}, u32[]{:S(2)}, u32[]{:S(2)}) %collective-permute-start) | collective-permute-done | bytes 262176 | tf_op jit(solution)/shard_map/ppermute | solution.py:15
  36.1 1.3 convolution_add_fusion.2
  37.3 4.3 %collective-permute-start.1 = (bf16[128,1024]{0,1:T(8,128)(2,1)S(1)}, bf16[128,1024]{0,1:T(8,128)(2,1)S(1)}, u32[]{:S(2)}, u32[]{:S(2)}) collective-permute-start(bf16[128,1024]{0,1:T(8,128)(2,1)S(1)} %collective-permute-done), channel_id=1, source_target_pairs={{0,6},{2,0},{4,2},{6,4},{1,7},{3,1},{5,3},{7,5},{8,14},{10,8},{12,... | collective-permute-start | bytes 786440 | tf_op jit(solution)/shard_map/ppermute | solution.py:15
  42.5 0.9 maximum_add_fusion
  43.4 5.0 %collective-permute-done.1 = bf16[128,1024]{0,1:T(8,128)(2,1)S(1)} collective-permute-done((bf16[128,1024]{0,1:T(8,128)(2,1)S(1)}, bf16[128,1024]{0,1:T(8,128)(2,1)S(1)}, u32[]{:S(2)}, u32[]{:S(2)}) %collective-permute-start.1) | collective-permute-done | bytes 262176 | tf_op jit(solution)/shard_map/ppermute | solution.py:15
  49.2 4.3 %collective-permute-start.2 = (bf16[128,1024]{0,1:T(8,128)(2,1)S(1)}, bf16[128,1024]{0,1:T(8,128)(2,1)S(1)}, u32[]{:S(2)}, u32[]{:S(2)}) collective-permute-start(bf16[128,1024]{0,1:T(8,128)(2,1)S(1)} %collective-permute-done.1), channel_id=1, source_target_pairs={{0,6},{2,0},{4,2},{6,4},{1,7},{3,1},{5,3},{7,5},{8,14},{10,8},{12,... | collective-permute-start | bytes 786440 | tf_op jit(solution)/shard_map/ppermute | solution.py:15
  54.2 0.9 copy.136
  55.1 8.0 %collective-permute-done.2 = bf16[128,1024]{0,1:T(8,128)(2,1)S(1)} collective-permute-done((bf16[128,1024]{0,1:T(8,128)(2,1)S(1)}, bf16[128,1024]{0,1:T(8,128)(2,1)S(1)}, u32[]{:S(2)}, u32[]{:S(2)}) %collective-permute-start.2) | collective-permute-done | bytes 262176 | tf_op jit(solution)/shard_map/ppermute | solution.py:15
  63.2 1.1 fusion.6
  64.6 0.8 copy.142
  65.5 2.0 %maximum_add_fusion.1 = f32[128,1024]{1,0:T(8,128)} fusion(f32[128,1024]{1,0:T(8,128)} %collective-permute-done.4, f32[128,512]{1,0:T(8,128)S(1)} %copy.137, f32[128,512]{1,0:T(8,128)} %copy.136), kind=kLoop, calls=%fused_computation.54 | loop fusion | flops 262144 | bytes 1572864 | tf_op jit(solution)/shard_map/add | solution.py:142
  67.4 4.3 %collective-permute-start.5 = (f32[128,1024]{1,0:T(8,128)}, f32[128,1024]{1,0:T(8,128)}, u32[]{:S(2)}, u32[]{:S(2)}) collective-permute-start(f32[128,1024]{1,0:T(8,128)} %maximum_add_fusion.1), channel_id=1, source_target_pairs={{0,6},{2,0},{4,2},{6,4},{1,7},{3,1},{5,3},{7,5},{8,14},{10,8},{12,... | collective-permute-start | bytes 1572872 | tf_op jit(solution)/shard_map/ppermute | solution.py:15
  72.5 8.9 %collective-permute-done.5 = f32[128,1024]{1,0:T(8,128)} collective-permute-done((f32[128,1024]{1,0:T(8,128)}, f32[128,1024]{1,0:T(8,128)}, u32[]{:S(2)}, u32[]{:S(2)}) %collective-permute-start.5) | collective-permute-done | bytes 524320 | tf_op jit(solution)/shard_map/ppermute | solution.py:15
  81.4 1.9 %maximum_add_fusion.2 = f32[128,1024]{1,0:T(8,128)} fusion(f32[128,1024]{1,0:T(8,128)} %collective-permute-done.5, f32[128,512]{1,0:T(8,128)S(1)} %copy-done.1, f32[128,512]{1,0:T(8,128)S(1)} %copy.141), kind=kLoop, calls=%fused_computation.55 | loop fusion | flops 262144 | bytes 1572864 | tf_op jit(solution)/shard_map/add | solution.py:142
  83.3 4.3 %collective-permute-start.6 = (f32[128,1024]{1,0:T(8,128)}, f32[128,1024]{1,0:T(8,128)}, u32[]{:S(2)}, u32[]{:S(2)}) collective-permute-start(f32[128,1024]{1,0:T(8,128)} %maximum_add_fusion.2), channel_id=1, source_target_pairs={{0,6},{2,0},{4,2},{6,4},{1,7},{3,1},{5,3},{7,5},{8,14},{10,8},{12,... | collective-permute-start | bytes 1572872 | tf_op jit(solution)/shard_map/ppermute | solution.py:15
  88.6 7.7 %collective-permute-done.6 = f32[128,1024]{1,0:T(8,128)} collective-permute-done((f32[128,1024]{1,0:T(8,128)}, f32[128,1024]{1,0:T(8,128)}, u32[]{:S(2)}, u32[]{:S(2)}) %collective-permute-start.6) | collective-permute-done | bytes 524320 | tf_op jit(solution)/shard_map/ppermute | solution.py:15
  96.3 1.1 convert_element_type.131
  97.5 1.3 collective-permute-start.7
  98.8 1.1 slice_reduce_fusion
  99.9 38.1 %all-reduce = (f32[1,2048]{1,0:T(1,128)}, f32[1,512]{1,0:T(1,128)}, f32[1,512]{1,0:T(1,128)}) all-reduce(f32[1,2048]{1,0:T(1,128)S(1)} %bitcast.275, f32[1,512]{1,0:T(1,128)S(1)} %bitcast.279, f32[1,512]{1,0:T(1,128)S(1)} %bitcast.278), channel_id=1, replica_groups=mesh['section'=4,'ctx'=4,'dp'=2] {'ctx','dp'}, use_global_device_ids=true, to_apply=%region_2.3 | all-reduce | flops 3072 | bytes 24576 | tf_op jit(solution)/shard_map/psum | solution.py:146
  (77 shorter events, 14.0 us)
Async XLA Ops:
  0.7 1.9 %copy-start.2 = (bf16[1,1,128,2048]{3,2,1,0:T(8,128)(2,1)S(1)}, bf16[1,1,128,2048]{3,2,1,0:T(8,128)(2,1)}, u32[]{:S(2)}) copy-start(bf16[1,1,128,2048]{3,2,1,0:T(8,128)(2,1)} %param.9) | copy-start | bytes 1572868
  2.6 0.7 copy-start.10
  2.6 0.8 copy-start.11
  2.6 0.9 copy-start.4
  3.3 1.5 %copy-start.3 = (f32[1,1,16,128]{3,2,1,0:T(8,128)S(1)}, f32[1,1,16,128]{3,2,1,0:T(8,128)}, u32[]{:S(2)}) copy-start(f32[1,1,16,128]{3,2,1,0:T(8,128)} %param.14) | copy-start | bytes 24580
  3.6 1.3 copy-start.8
  8.6 2.1 %copy-start.5 = (bf16[1,1,128,512]{3,2,1,0:T(8,128)(2,1)S(1)}, bf16[1,1,128,512]{3,2,1,0:T(8,128)(2,1)}, u32[]{:S(2)}) copy-start(bf16[1,1,128,512]{3,2,1,0:T(8,128)(2,1)} %param.11) | copy-start | bytes 393220
  12.2 6.0 %copy-start.9 = (f32[1,512]{1,0:T(1,128)S(1)}, f32[1,512]{1,0:T(1,128)}, u32[]{:S(2)}) copy-start(f32[1,512]{1,0:T(1,128)} %copy-done.8) | copy-start | bytes 6148
  13.2 29.3 %collective-permute-start.3 = (f32[128,1024]{1,0:T(8,128)}, f32[128,1024]{1,0:T(8,128)S(1)}, u32[]{:S(2)}, u32[]{:S(2)}) collective-permute-start(f32[128,1024]{1,0:T(8,128)} %pad_maximum_fusion.1), channel_id=1, source_target_pairs={{0,6},{2,0},{4,2},{6,4},{1,7},{3,1},{5,3},{7,5},{8,14},{10,8},{12,... | collective-permute-start | bytes 1572872 | tf_op jit(solution)/shard_map/ppermute | solution.py:15
  18.5 16.8 %copy-start.7 = (pred[128,128]{0,1:T(8,128)(4,1)S(1)}, pred[128,128]{0,1:T(8,128)(4,1)}, u32[]{:S(2)}) copy-start(pred[128,128]{0,1:T(8,128)(4,1)} %get-tuple-element.22) | copy-start | bytes 49156
  18.5 16.8 %collective-permute-start = (bf16[128,1024]{0,1:T(8,128)(2,1)S(1)}, bf16[128,1024]{0,1:T(8,128)(2,1)S(1)}, u32[]{:S(2)}, u32[]{:S(2)}) collective-permute-start(bf16[128,1024]{0,1:T(8,128)(2,1)S(1)} %pad_maximum_fusion.2), channel_id=1, source_target_pairs={{0,6},{2,0},{4,2},{6,4},{1,7},{3,1},{5,3},{7,5},{8,14},{10,8},{12,... | collective-permute-start | bytes 786440 | tf_op jit(solution)/shard_map/ppermute | solution.py:15
  37.3 11.0 %collective-permute-start.1 = (bf16[128,1024]{0,1:T(8,128)(2,1)S(1)}, bf16[128,1024]{0,1:T(8,128)(2,1)S(1)}, u32[]{:S(2)}, u32[]{:S(2)}) collective-permute-start(bf16[128,1024]{0,1:T(8,128)(2,1)S(1)} %collective-permute-done), channel_id=1, source_target_pairs={{0,6},{2,0},{4,2},{6,4},{1,7},{3,1},{5,3},{7,5},{8,14},{10,8},{12,... | collective-permute-start | bytes 786440 | tf_op jit(solution)/shard_map/ppermute | solution.py:15
  42.5 5.9 %copy-start.6 = (pred[128,128]{0,1:T(8,128)(4,1)S(1)}, pred[128,128]{0,1:T(8,128)(4,1)}, u32[]{:S(2)}) copy-start(pred[128,128]{0,1:T(8,128)(4,1)} %get-tuple-element.23) | copy-start | bytes 49156
  43.4 22.1 %collective-permute-start.4 = (f32[128,1024]{1,0:T(8,128)}, f32[128,1024]{1,0:T(8,128)}, u32[]{:S(2)}, u32[]{:S(2)}) collective-permute-start(f32[128,1024]{1,0:T(8,128)} %maximum_add_fusion), channel_id=1, source_target_pairs={{0,6},{2,0},{4,2},{6,4},{1,7},{3,1},{5,3},{7,5},{8,14},{10,8},{12,... | collective-permute-start | bytes 1572872 | tf_op jit(solution)/shard_map/ppermute | solution.py:15
  49.2 14.0 %collective-permute-start.2 = (bf16[128,1024]{0,1:T(8,128)(2,1)S(1)}, bf16[128,1024]{0,1:T(8,128)(2,1)S(1)}, u32[]{:S(2)}, u32[]{:S(2)}) collective-permute-start(bf16[128,1024]{0,1:T(8,128)(2,1)S(1)} %collective-permute-done.1), channel_id=1, source_target_pairs={{0,6},{2,0},{4,2},{6,4},{1,7},{3,1},{5,3},{7,5},{8,14},{10,8},{12,... | collective-permute-start | bytes 786440 | tf_op jit(solution)/shard_map/ppermute | solution.py:15
  67.4 14.0 %collective-permute-start.5 = (f32[128,1024]{1,0:T(8,128)}, f32[128,1024]{1,0:T(8,128)}, u32[]{:S(2)}, u32[]{:S(2)}) collective-permute-start(f32[128,1024]{1,0:T(8,128)} %maximum_add_fusion.1), channel_id=1, source_target_pairs={{0,6},{2,0},{4,2},{6,4},{1,7},{3,1},{5,3},{7,5},{8,14},{10,8},{12,... | collective-permute-start | bytes 1572872 | tf_op jit(solution)/shard_map/ppermute | solution.py:15
  72.0 9.3 %copy-start.1 = (f32[128,512]{1,0:T(8,128)S(1)}, f32[128,512]{1,0:T(8,128)}, u32[]{:S(2)}) copy-start(f32[128,512]{1,0:T(8,128)} %copy.142) | copy-start | bytes 786436
  72.4 15.2 %copy-start = (f32[4,128,4,128]{3,1,2,0:T(8,128)S(1)}, f32[4,128,4,128]{3,1,2,0:T(8,128)}, u32[]{:S(2)}) copy-start(f32[4,128,4,128]{3,1,2,0:T(8,128)} %convolution_add_fusion.2) | copy-start | bytes 3145732
  83.3 13.1 %collective-permute-start.6 = (f32[128,1024]{1,0:T(8,128)}, f32[128,1024]{1,0:T(8,128)}, u32[]{:S(2)}, u32[]{:S(2)}) collective-permute-start(f32[128,1024]{1,0:T(8,128)} %maximum_add_fusion.2), channel_id=1, source_target_pairs={{0,6},{2,0},{4,2},{6,4},{1,7},{3,1},{5,3},{7,5},{8,14},{10,8},{12,... | collective-permute-start | bytes 1572872 | tf_op jit(solution)/shard_map/ppermute | solution.py:15
  97.5 40.5 %collective-permute-start.7 = (bf16[128,3072]{1,0:T(8,128)(2,1)S(1)}, bf16[128,3072]{1,0:T(8,128)(2,1)S(1)}, u32[]{:S(2)}, u32[]{:S(2)}) collective-permute-start(bf16[128,3072]{1,0:T(8,128)(2,1)S(1)} %pad_maximum_fusion), channel_id=1, source_target_pairs={{8,0},{16,8},{24,16},{9,1},{17,9},{25,17},{10,2},{18,10},{26,18},{... | collective-permute-start | bytes 2359304 | tf_op jit(solution)/shard_map/ppermute | solution.py:21
where the time goes:
time: 140 us; the launch traced here: 139 us
  waiting for transfers between devices  45.6 us (33%)
  blocking collectives  38.1 us (27%)
  starting transfers between devices  24 us (17%)
  other arithmetic  11.7 us (8%)
  local copies, waits for them, and re-layouts  10.4 us (7%)
  matrix products  8.49 us (6%)
    ppermute x7, waiting for transfers between devices, passed_along(): lax.ppermute(value, axis, [(i, (i + by) % size) for i in range(size)])  45.6 us
    psum x1, blocking collectives, body(): lax.psum((jnp.sum(grad_q, axis=0, keepdims=True), jnp.sum(kv_grads[:, :ke...  38.1 us
    ppermute x7, starting transfers between devices, passed_along(): lax.ppermute(value, axis, [(i, (i + by) % size) for i in range(size)])  22.7 us
    add x3, other arithmetic, body(): kv_grads = kv_grads + kv_terms  4.71 us
    convert_element_type x1, local copies, waits for them, and re-layouts, body(): output_grouped.astype(jnp.float32)  2.87 us
  transfers between devices with their start and end apart: 8, of which 5 were waited for; matrix products, arithmetic and copies ran while one was open for 8% of the time, Pallas kernels for 0%

commit v1 on v0

v1 whole, which is shorter than its diff:
```python
import functools
import math

import jax
import jax.numpy as jnp
from jax import lax
from jax.experimental import pallas as pl
from jax.experimental.pallas import tpu as pltpu
from jax.sharding import PartitionSpec as P

QUERY_HEADS = 16
KEY_VALUE_HEADS = 4
HEAD_SIZE = 128
GROUP = QUERY_HEADS // KEY_VALUE_HEADS
GROUP_WIDTH = GROUP * HEAD_SIZE
MESH = pl.DeviceIdType.MESH
NT = (((1,), (1,)), ((), ()))
NN = (((1,), (0,)), ((), ()))


def partner(me, step, size):
    if size == 4:
        high, low = me // 2, me % 2
        high = 1 - high if step // 2 else high
        low = 1 - low if step % 2 else low
        return 2 * high + low
    return (me + step) % size


def kernel(
    n_section,
    n_ctx,
    n_dp,
    q_ref,
    k_ref,
    v_ref,
    o_ref,
    g_ref,
    lse_ref,
    bq_ref,
    bk_ref,
    bv_ref,
    rq_ref,
    rk_ref,
    rv_ref,
    sum_q_ref,
    sum_k_ref,
    sum_v_ref,
    q_in,
    g_in,
    k_in,
    v_in,
    rows_in,
    rows_out,
    o_own,
    g_own,
    bias,
    k_all,
    v_all,
    k_turned,
    grad_k,
    grad_v,
    grad_q_turned,
    q_stack,
    g_stack,
    q_out,
    k_out,
    v_out,
    sums,
    in_send,
    in_recv,
    out_send,
    out_recv,
    sum_send,
    sum_recv,
    local_sem,
):
    tokens = q_in.shape[1]
    half = tokens // 2
    scale = 1.0 / math.sqrt(HEAD_SIZE)
    section = lax.axis_index("section")
    me = lax.axis_index("ctx")
    replica = lax.axis_index("dp")
    everyone = n_ctx * n_dp
    my_place = replica * n_ctx + me
    has_before = section > 0
    has_after = section < n_section - 1

    def ctx_device(ctx):
        return {"section": section, "ctx": ctx, "dp": replica}

    def before_device(ctx):
        return {"section": section - 1, "ctx": ctx, "dp": replica}

    def after_device(ctx):
        return {"section": section + 1, "ctx": ctx, "dp": replica}

    def place_device(place):
        return {"section": section, "ctx": place % n_ctx, "dp": place // n_ctx}

    def group_columns(ctx, width):
        return pl.ds(pl.multiple_of(ctx * width, width), width)

    def sources(ctx):
        wide, narrow = group_columns(ctx, GROUP_WIDTH), group_columns(ctx, HEAD_SIZE)
        return (
            (k_ref.at[0, 0, :, narrow], k_in),
            (v_ref.at[0, 0, :, narrow], v_in),
            (q_ref.at[0, 0, :, wide], q_in),
            (g_ref.at[0, 0, :, wide], g_in),
            (rows_out.at[ctx], rows_in),
        )

    def in_copy(item, to, slot):
        source, target = sources(to)[item]
        return pltpu.make_async_remote_copy(
            src_ref=source,
            dst_ref=target.at[slot],
            send_sem=in_send.at[to, item],
            recv_sem=in_recv.at[slot, item],
            device_id=ctx_device(to),
            device_id_type=MESH,
        )

    def own_copy(item):
        source, target = sources(me)[item]
        return pltpu.make_async_copy(source, target.at[me], local_sem.at[item])

    def out_copies(ctx, slot):
        wide, narrow = group_columns(slot, GROUP_WIDTH), group_columns(slot, HEAD_SIZE)
        return [
            pltpu.make_async_remote_copy(
                src_ref=source.at[ctx],
                dst_ref=target,
                send_sem=out_send.at[ctx, item],
                recv_sem=out_recv.at[slot, item],
                device_id=before_device(ctx),
                device_id_type=MESH,
            )
            for item, (source, target) in enumerate(
                (
                    (q_out, rq_ref.at[0, 0, :, wide]),
                    (k_out, rk_ref.at[0, 0, :, narrow]),
                    (v_out, rv_ref.at[0, 0, :, narrow]),
                )
            )
        ]

    def sum_copy(place, slot):
        return pltpu.make_async_remote_copy(
            src_ref=sums.at[my_place],
            dst_ref=sums.at[slot],
            send_sem=sum_send.at[place],
            recv_sem=sum_recv.at[slot],
            device_id=place_device(place),
            device_id_type=MESH,
        )

    o_copy = pltpu.make_async_copy(o_ref.at[0, 0], o_own, local_sem.at[4])
    g_copy = pltpu.make_async_copy(g_ref.at[0, 0], g_own, local_sem.at[5])

    barrier = pltpu.get_barrier_semaphore()
    for step in range(1, everyone):
        pl.semaphore_signal(
            barrier,
            inc=1,
            device_id=place_device((my_place + step) % everyone),
            device_id_type=MESH,
        )

    @pl.when(has_before)
    def _():
        for ctx in range(n_ctx):
            pl.semaphore_signal(barrier, inc=1, device_id=before_device(ctx), device_id_type=MESH)

    @pl.when(has_after)
    def _():
        for ctx in range(n_ctx):
            pl.semaphore_signal(barrier, inc=1, device_id=after_device(ctx), device_id_type=MESH)

    o_copy.start()
    g_copy.start()
    for item in range(4):
        own_copy(item).start()
    bias[:, :GROUP_WIDTH] = jnp.zeros((8, GROUP_WIDTH), jnp.float32)

    neighbours = jnp.where(has_before, n_ctx, 0) + jnp.where(has_after, n_ctx, 0)
    pl.semaphore_wait(barrier, everyone - 1 + neighbours)

    for items in ((0, 1), (2, 3)):
        for step in reversed(range(1, n_ctx)):
            for item in items:
                in_copy(item, partner(me, step, n_ctx), me).start()

    o_copy.wait()
    g_copy.wait()
    for group in range(KEY_VALUE_HEADS):
        lines = [lse_ref[0, 0, pl.ds(group * GROUP, GROUP), :]]
        for head in range(group * GROUP, (group + 1) * GROUP):
            columns = slice(head * HEAD_SIZE, (head + 1) * HEAD_SIZE)
            product = g_own[:, columns].astype(jnp.float32) * o_own[:, columns].astype(jnp.float32)
            lines.append(jnp.sum(product.T, axis=0, keepdims=True))
        rows_out[group] = jnp.concatenate(lines, axis=0)
    for step in reversed(range(1, n_ctx)):
        in_copy(4, partner(me, step, n_ctx), me).start()
    rows_in[me] = rows_out[me]

    for ctx in range(n_ctx):
        wide = slice(ctx * GROUP_WIDTH, (ctx + 1) * GROUP_WIDTH)
        narrow = slice(ctx * HEAD_SIZE, (ctx + 1) * HEAD_SIZE)

        @pl.when(me == ctx)
        def _():
            bias[0:1, :] = bq_ref[:, wide].astype(jnp.float32)
            bias[1:2, :HEAD_SIZE] = bk_ref[:, narrow].astype(jnp.float32)
            bias[2:3, :HEAD_SIZE] = bv_ref[:, narrow].astype(jnp.float32)

    for item in range(4):
        own_copy(item).wait()
    for step in range(1, n_ctx):
        for item in (0, 1):
            in_copy(item, partner(me, step, n_ctx), partner(me, step, n_ctx)).wait_recv()
    for ctx in range(n_ctx):
        k_low = (k_in[ctx].astype(jnp.float32) + bias[1:2, :HEAD_SIZE]).astype(jnp.bfloat16)
        k_all[ctx] = k_low
        k_turned[ctx] = k_low.astype(jnp.float32).T.astype(jnp.bfloat16)
        v_all[ctx] = (v_in[ctx].astype(jnp.float32) + bias[2:3, :HEAD_SIZE]).astype(jnp.bfloat16)
    grad_k[...] = jnp.zeros_like(grad_k)
    grad_v[...] = jnp.zeros_like(grad_v)

    def positions(block, local):
        late = (2 * n_ctx - 1 - block) * half + local - half
        return jnp.where(local < half, block * half + local, late)

    q_local = jnp.concatenate(
        [lax.broadcasted_iota(jnp.int32, (1, tokens), 1)] * GROUP, axis=1
    )
    k_local = lax.broadcasted_iota(jnp.int32, (tokens, 1), 0)
    head_sums = [jnp.zeros((1, HEAD_SIZE), jnp.float32) for _ in range(GROUP)]

    for step in range(n_ctx):
        block = partner(me, step, n_ctx)
        if step:
            for item in (2, 3, 4):
                in_copy(item, block, block).wait_recv()
        for head in range(GROUP):
            columns = slice(head * HEAD_SIZE, (head + 1) * HEAD_SIZE)
            rows = slice(head * tokens, (head + 1) * tokens)
            q_stack[rows] = (
                q_in[block, :, columns].astype(jnp.float32) + bias[0:1, columns]
            ).astype(jnp.bfloat16)
            g_stack[rows] = g_in[block, :, columns]
        grad_q_turned[...] = jnp.zeros_like(grad_q_turned)
        lines = rows_in[block]
        lse_line = jnp.concatenate([lines[h : h + 1] for h in range(GROUP)], axis=1)
        delta_line = jnp.concatenate([lines[GROUP + h : GROUP + h + 1] for h in range(GROUP)], axis=1)
        q_pos = positions(block, q_local)

        def over_keys(owner, _):
            queries, gradients = q_stack[...], g_stack[...]
            scores = lax.dot_general(
                k_all[owner], queries, NT, preferred_element_type=jnp.float32
            )
            causal = positions(owner, k_local) <= q_pos
            prob = jnp.where(causal, jnp.exp(scores * scale - lse_line), 0.0)
            grad_prob = lax.dot_general(
                v_all[owner], gradients, NT, preferred_element_type=jnp.float32
            )
            score_low = (prob * (grad_prob - delta_line)).astype(jnp.bfloat16)
            prob_low = prob.astype(jnp.bfloat16)
            grad_v[owner] += lax.dot_general(
                prob_low, gradients, NN, preferred_element_type=jnp.float32
            )
            grad_k[owner] += lax.dot_general(
                score_low, queries, NN, preferred_element_type=jnp.float32
            )
            grad_q_turned[...] += lax.dot_general(
                k_turned[owner], score_low, NN, preferred_element_type=jnp.float32
            )
            return 0

        lax.fori_loop(0, n_ctx, over_keys, 0)
        for head in range(GROUP):
            grad_q = grad_q_turned[:, head * tokens : (head + 1) * tokens].T * scale
            head_sums[head] += jnp.sum(grad_q, axis=0, keepdims=True)
            q_out[block, :, head * HEAD_SIZE : (head + 1) * HEAD_SIZE] = grad_q.astype(jnp.bfloat16)

        @pl.when(has_before)
        def _():
            out_copies(block, me)[0].start()

    key_sum = jnp.zeros((1, HEAD_SIZE), jnp.float32)
    value_sum = jnp.zeros((1, HEAD_SIZE), jnp.float32)
    for ctx in range(n_ctx):
        key_part = grad_k[ctx] * scale
        k_out[ctx] = key_part.astype(jnp.bfloat16)
        v_out[ctx] = grad_v[ctx].astype(jnp.bfloat16)
        key_sum += jnp.sum(key_part, axis=0, keepdims=True)
        value_sum += jnp.sum(grad_v[ctx], axis=0, keepdims=True)
    blank = jnp.zeros((8 - GROUP - 2, HEAD_SIZE), jnp.float32)
    sums[my_place] = jnp.concatenate(head_sums + [key_sum, value_sum, blank], axis=0)
    for step in range(1, everyone):
        place = (my_place + step) % everyone
        sum_copy(place, my_place).start()

    @pl.when(has_before)
    def _():
        for step in reversed(range(n_ctx)):
            for copy in out_copies(partner(me, step, n_ctx), me)[1:]:
                copy.start()

    @pl.when(section == n_section - 1)
    def _():
        o_own[...] = jnp.zeros_like(o_own)
        blanks = [
            pltpu.make_async_copy(o_own, rq_ref.at[0, 0], local_sem.at[0]),
            pltpu.make_async_copy(
                o_own.at[:, : KEY_VALUE_HEADS * HEAD_SIZE], rk_ref.at[0, 0], local_sem.at[1]
            ),
            pltpu.make_async_copy(
                o_own.at[:, : KEY_VALUE_HEADS * HEAD_SIZE], rv_ref.at[0, 0], local_sem.at[2]
            ),
        ]
        for copy in blanks:
            copy.start()
        for copy in blanks:
            copy.wait()

    for step in range(1, everyone):
        place = (my_place + step) % everyone
        sum_copy(place, place).wait_recv()
    for ctx in range(n_ctx):
        total = sums[ctx]
        for other in range(1, n_dp):
            total += sums[other * n_ctx + ctx]
        for head in range(GROUP):
            start = ctx * GROUP_WIDTH + head * HEAD_SIZE
            sum_q_ref[:, start : start + HEAD_SIZE] = total[head : head + 1]
        narrow = slice(ctx * HEAD_SIZE, (ctx + 1) * HEAD_SIZE)
        sum_k_ref[:, narrow] = total[GROUP : GROUP + 1]
        sum_v_ref[:, narrow] = total[GROUP + 1 : GROUP + 2]

    for step in range(1, n_ctx):
        for item in range(5):
            in_copy(item, partner(me, step, n_ctx), me).wait_send()
    for step in range(1, everyone):
        sum_copy((my_place + step) % everyone, my_place).wait_send()

    @pl.when(has_before)
    def _():
        for ctx in range(n_ctx):
            for copy in out_copies(ctx, me):
                copy.wait_send()

    @pl.when(has_after)
    def _():
        for ctx in range(n_ctx):
            for copy in out_copies(ctx, ctx):
                copy.wait_recv()


def solution(mesh):
    n_section, n_ctx, n_dp = mesh.shape["section"], mesh.shape["ctx"], mesh.shape["dp"]
    assert n_ctx == KEY_VALUE_HEADS

    def body(q_in, key_in, value_in, out_saved, out_grad, lse, bias_q, key_bias, value_bias):
        tokens = q_in.shape[2]
        width_q, width_k = QUERY_HEADS * HEAD_SIZE, KEY_VALUE_HEADS * HEAD_SIZE
        everyone = n_ctx * n_dp
        anywhere = pl.BlockSpec(memory_space=pl.ANY)
        vmem = pl.BlockSpec(memory_space=pltpu.VMEM)
        low, full = jnp.bfloat16, jnp.float32
        return pl.pallas_call(
            functools.partial(kernel, n_section, n_ctx, n_dp),
            out_shape=(
                jax.ShapeDtypeStruct((1, 1, tokens, width_q), low),
                jax.ShapeDtypeStruct((1, 1, tokens, width_k), low),
                jax.ShapeDtypeStruct((1, 1, tokens, width_k), low),
                jax.ShapeDtypeStruct((1, width_q), full),
                jax.ShapeDtypeStruct((1, width_k), full),
                jax.ShapeDtypeStruct((1, width_k), full),
            ),
            in_specs=[anywhere] * 5 + [vmem] * 4,
            out_specs=(anywhere, anywhere, anywhere, vmem, vmem, vmem),
            scratch_shapes=[
                pltpu.VMEM((n_ctx, tokens, GROUP_WIDTH), low),
                pltpu.VMEM((n_ctx, tokens, GROUP_WIDTH), low),
                pltpu.VMEM((n_ctx, tokens, HEAD_SIZE), low),
                pltpu.VMEM((n_ctx, tokens, HEAD_SIZE), low),
                pltpu.VMEM((n_ctx, 2 * GROUP, tokens), full),
                pltpu.VMEM((n_ctx, 2 * GROUP, tokens), full),
                pltpu.VMEM((tokens, width_q), low),
                pltpu.VMEM((tokens, width_q), low),
                pltpu.VMEM((8, GROUP_WIDTH), full),
                pltpu.VMEM((n_ctx, tokens, HEAD_SIZE), low),
                pltpu.VMEM((n_ctx, tokens, HEAD_SIZE), low),
                pltpu.VMEM((n_ctx, HEAD_SIZE, tokens), low),
                pltpu.VMEM((n_ctx, tokens, HEAD_SIZE), full),
                pltpu.VMEM((n_ctx, tokens, HEAD_SIZE), full),
                pltpu.VMEM((HEAD_SIZE, GROUP * tokens), full),
                pltpu.VMEM((GROUP * tokens, HEAD_SIZE), low),
                pltpu.VMEM((GROUP * tokens, HEAD_SIZE), low),
                pltpu.VMEM((n_ctx, tokens, GROUP_WIDTH), low),
                pltpu.VMEM((n_ctx, tokens, HEAD_SIZE), low),
                pltpu.VMEM((n_ctx, tokens, HEAD_SIZE), low),
                pltpu.VMEM((everyone, 8, HEAD_SIZE), full),
                pltpu.SemaphoreType.DMA((n_ctx, 5)),
                pltpu.SemaphoreType.DMA((n_ctx, 5)),
                pltpu.SemaphoreType.DMA((n_ctx, 3)),
                pltpu.SemaphoreType.DMA((n_ctx, 3)),
                pltpu.SemaphoreType.DMA((everyone,)),
                pltpu.SemaphoreType.DMA((everyone,)),
                pltpu.SemaphoreType.DMA((6,)),
            ],
            compiler_params=pltpu.CompilerParams(
                collective_id=0, has_side_effects=True, vmem_limit_bytes=40 * 1024 * 1024
            ),
        )(q_in, key_in, value_in, out_saved, out_grad, lse, bias_q, key_bias, value_bias)

    rows = P("dp", "section", "ctx", None)
    line = P("section", None)
    return jax.shard_map(
        body,
        mesh=mesh,
        in_specs=(rows,) * 5 + (P("dp", "section", None, "ctx"),) + (line,) * 3,
        out_specs=(rows,) * 3 + (line,) * 3,
        check_vma=False,
    )
```

time: 140 us -> 66.8 us (0.48)
  the two profiles are of different devices: /device:TPU:0 before, /device:TPU:1 now
where the time goes in v1:
time: 66.8 us; the launch traced here: 66.4 us
  Pallas kernels  54.2 us (81%)
  local copies, waits for them, and re-layouts  11.5 us (17%)
    pallas_call x1, Pallas kernels, body(): pl.pallas_call(functools.partial(kernel, n_section, n_ctx, n_dp), out_sha...  54.2 us
    unnamed x24, local copies, waits for them, and re-layouts  11.5 us

profile of v1, /device:TPU:1, one launch (start us, length us, event | category | flops | bytes accessed | tf_op | source)
XLA Modules:
  0.0 66.4 jit_solution(14517221884381078893)
XLA Ops:
  0.6 0.0 copy-start
  0.6 1.0 %copy-done = bf16[1,1,128,2048]{3,2,1,0:T(8,128)(2,1)S(1)} copy-done((bf16[1,1,128,2048]{3,2,1,0:T(8,128)(2,1)S(1)}, bf16[1,1,128,2048]{3,2,1,0:T(8,128)(2,1)}, u32[]{:S(2)}) %copy-start) | copy-done | bytes 524312
  1.7 0.0 copy-start.1
  1.7 1.0 %copy-done.1 = bf16[1,1,128,2048]{3,2,1,0:T(8,128)(2,1)S(1)} copy-done((bf16[1,1,128,2048]{3,2,1,0:T(8,128)(2,1)S(1)}, bf16[1,1,128,2048]{3,2,1,0:T(8,128)(2,1)}, u32[]{:S(2)}) %copy-start.1) | copy-done | bytes 524312
  2.7 0.0 copy-start.2
  2.7 1.0 %copy-done.2 = bf16[1,1,128,2048]{3,2,1,0:T(8,128)(2,1)S(1)} copy-done((bf16[1,1,128,2048]{3,2,1,0:T(8,128)(2,1)S(1)}, bf16[1,1,128,2048]{3,2,1,0:T(8,128)(2,1)}, u32[]{:S(2)}) %copy-start.2) | copy-done | bytes 524312
  3.8 0.0 copy-start.3
  3.8 0.9 %copy-done.3 = bf16[1,1,128,512]{3,2,1,0:T(8,128)(2,1)S(1)} copy-done((bf16[1,1,128,512]{3,2,1,0:T(8,128)(2,1)S(1)}, bf16[1,1,128,512]{3,2,1,0:T(8,128)(2,1)}, u32[]{:S(2)}) %copy-start.3) | copy-done | bytes 131096
  4.7 0.0 copy-start.4
  4.7 0.9 %copy-done.4 = bf16[1,1,128,512]{3,2,1,0:T(8,128)(2,1)S(1)} copy-done((bf16[1,1,128,512]{3,2,1,0:T(8,128)(2,1)S(1)}, bf16[1,1,128,512]{3,2,1,0:T(8,128)(2,1)}, u32[]{:S(2)}) %copy-start.4) | copy-done | bytes 131096
  5.6 0.0 copy-start.5
  5.6 0.7 %copy-done.5 = f32[1,1,16,128]{3,2,1,0:T(8,128)S(1)} copy-done((f32[1,1,16,128]{3,2,1,0:T(8,128)S(1)}, f32[1,1,16,128]{3,2,1,0:T(8,128)}, u32[]{:S(2)}) %copy-start.5) | copy-done | bytes 8216
  6.3 0.0 copy-start.6
  6.3 0.7 %copy-done.6 = bf16[1,2048]{1,0:T(2,128)(2,1)S(1)} copy-done((bf16[1,2048]{1,0:T(2,128)(2,1)S(1)}, bf16[1,2048]{1,0:T(2,128)(2,1)}, u32[]{:S(2)}) %copy-start.6) | copy-done | bytes 4120
  7.0 0.7 %copy-done.7 = bf16[1,512]{1,0:T(2,128)(2,1)S(1)} copy-done((bf16[1,512]{1,0:T(2,128)(2,1)S(1)}, bf16[1,512]{1,0:T(2,128)(2,1)}, u32[]{:S(2)}) %copy-start.7) | copy-done | bytes 1048
  7.6 0.0 copy-start.8
  7.7 0.7 %copy-done.8 = bf16[1,512]{1,0:T(2,128)(2,1)S(1)} copy-done((bf16[1,512]{1,0:T(2,128)(2,1)S(1)}, bf16[1,512]{1,0:T(2,128)(2,1)}, u32[]{:S(2)}) %copy-start.8) | copy-done | bytes 1048
  8.3 54.2 %shard_map.136 = (bf16[1,1,128,2048]{3,2,1,0:T(8,128)(2,1)S(1)}, bf16[1,1,128,512]{3,2,1,0:T(8,128)(2,1)S(1)}, bf16[1,1,128,512]{3,2,1,0:T(8,128)(2,1)S(1)}, f32...) custom-call(bf16[1,1,128,2048]{3,2,1,0:T(8,128)(2,1)S(1)} %copy-done, ...), custom_call_target="tpu_custom_call" | custom-call | tf_op jit(solution)/shard_map/pallas_call | solution.py:373
  62.5 0.8 %copy.21 = bf16[1,1,128,2048]{3,2,1,0:T(8,128)(2,1)} copy(bf16[1,1,128,2048]{3,2,1,0:T(8,128)(2,1)S(1)} %get-tuple-element.12) | data formatting | bytes 1048576
  63.3 0.7 copy.22
  64.0 0.7 copy.23
  64.7 0.6 copy.24
  65.2 0.6 copy.25
  65.8 0.6 copy.26
  (1 shorter events, 0.0 us)
Async XLA Ops:
  0.6 1.0 %copy-start = (bf16[1,1,128,2048]{3,2,1,0:T(8,128)(2,1)S(1)}, bf16[1,1,128,2048]{3,2,1,0:T(8,128)(2,1)}, u32[]{:S(2)}) copy-start(bf16[1,1,128,2048]{3,2,1,0:T(8,128)(2,1)} %q_ref.1) | copy-start | bytes 1572868
  1.7 1.0 %copy-start.1 = (bf16[1,1,128,2048]{3,2,1,0:T(8,128)(2,1)S(1)}, bf16[1,1,128,2048]{3,2,1,0:T(8,128)(2,1)}, u32[]{:S(2)}) copy-start(bf16[1,1,128,2048]{3,2,1,0:T(8,128)(2,1)} %o_ref.1) | copy-start | bytes 1572868
  2.7 1.0 %copy-start.2 = (bf16[1,1,128,2048]{3,2,1,0:T(8,128)(2,1)S(1)}, bf16[1,1,128,2048]{3,2,1,0:T(8,128)(2,1)}, u32[]{:S(2)}) copy-start(bf16[1,1,128,2048]{3,2,1,0:T(8,128)(2,1)} %g_ref.1) | copy-start | bytes 1572868
  3.8 0.9 %copy-start.3 = (bf16[1,1,128,512]{3,2,1,0:T(8,128)(2,1)S(1)}, bf16[1,1,128,512]{3,2,1,0:T(8,128)(2,1)}, u32[]{:S(2)}) copy-start(bf16[1,1,128,512]{3,2,1,0:T(8,128)(2,1)} %k_ref.1) | copy-start | bytes 393220
  4.7 0.9 %copy-start.4 = (bf16[1,1,128,512]{3,2,1,0:T(8,128)(2,1)S(1)}, bf16[1,1,128,512]{3,2,1,0:T(8,128)(2,1)}, u32[]{:S(2)}) copy-start(bf16[1,1,128,512]{3,2,1,0:T(8,128)(2,1)} %v_ref.1) | copy-start | bytes 393220
  5.6 0.7 %copy-start.5 = (f32[1,1,16,128]{3,2,1,0:T(8,128)S(1)}, f32[1,1,16,128]{3,2,1,0:T(8,128)}, u32[]{:S(2)}) copy-start(f32[1,1,16,128]{3,2,1,0:T(8,128)} %lse_ref.1) | copy-start | bytes 24580
  6.3 0.7 %copy-start.6 = (bf16[1,2048]{1,0:T(2,128)(2,1)S(1)}, bf16[1,2048]{1,0:T(2,128)(2,1)}, u32[]{:S(2)}) copy-start(bf16[1,2048]{1,0:T(2,128)(2,1)} %bq_ref.1) | copy-start | bytes 12292
  7.0 0.7 %copy-start.7 = (bf16[1,512]{1,0:T(2,128)(2,1)S(1)}, bf16[1,512]{1,0:T(2,128)(2,1)}, u32[]{:S(2)}) copy-start(bf16[1,512]{1,0:T(2,128)(2,1)} %bk_ref.1) | copy-start | bytes 3076
  7.6 0.7 %copy-start.8 = (bf16[1,512]{1,0:T(2,128)(2,1)S(1)}, bf16[1,512]{1,0:T(2,128)(2,1)}, u32[]{:S(2)}) copy-start(bf16[1,512]{1,0:T(2,128)(2,1)} %bv_ref.1) | copy-start | bytes 3076

commit v2 on v1

--- a/solution.py
+++ b/solution.py
@@ -36,10 +36,10 @@
     v_ref,
     o_ref,
     g_ref,
-    lse_ref,
-    bq_ref,
-    bk_ref,
-    bv_ref,
+    lse_far,
+    bq_far,
+    bk_far,
+    bv_far,
     rq_ref,
     rk_ref,
     rv_ref,
@@ -74,6 +74,10 @@
     sum_send,
     sum_recv,
     local_sem,
+    lse_ref,
+    bq_ref,
+    bk_ref,
+    bv_ref,
 ):
     tokens = q_in.shape[1]
     half = tokens // 2
@@ -159,6 +163,13 @@
     o_copy = pltpu.make_async_copy(o_ref.at[0, 0], o_own, local_sem.at[4])
     g_copy = pltpu.make_async_copy(g_ref.at[0, 0], g_own, local_sem.at[5])
 
+    small_copies = [
+        pltpu.make_async_copy(source, target, local_sem.at[6 + item])
+        for item, (source, target) in enumerate(
+            ((lse_far, lse_ref), (bq_far, bq_ref), (bk_far, bk_ref), (bv_far, bv_ref))
+        )
+    ]
+
     barrier = pltpu.get_barrier_semaphore()
     for step in range(1, everyone):
         pl.semaphore_signal(
@@ -180,6 +191,8 @@
 
     o_copy.start()
     g_copy.start()
+    for copy in small_copies:
+        copy.start()
     for item in range(4):
         own_copy(item).start()
     bias[:, :GROUP_WIDTH] = jnp.zeros((8, GROUP_WIDTH), jnp.float32)
@@ -194,6 +207,8 @@
 
     o_copy.wait()
     g_copy.wait()
+    for copy in small_copies:
+        copy.wait()
     for group in range(KEY_VALUE_HEADS):
         lines = [lse_ref[0, 0, pl.ds(group * GROUP, GROUP), :]]
         for head in range(group * GROUP, (group + 1) * GROUP):
@@ -359,6 +374,18 @@
                 copy.wait_recv()
 
 
+def placing(*refs):
+    sources, targets, sems = refs[:6], refs[6:12], refs[12]
+    copies = [
+        pltpu.make_async_copy(source, target, sems.at[item])
+        for item, (source, target) in enumerate(zip(sources, targets))
+    ]
+    for copy in copies:
+        copy.start()
+    for copy in copies:
+        copy.wait()
+
+
 def solution(mesh):
     n_section, n_ctx, n_dp = mesh.shape["section"], mesh.shape["ctx"], mesh.shape["dp"]
     assert n_ctx == KEY_VALUE_HEADS
@@ -369,8 +396,9 @@
         everyone = n_ctx * n_dp
         anywhere = pl.BlockSpec(memory_space=pl.ANY)
         vmem = pl.BlockSpec(memory_space=pltpu.VMEM)
+        hbm = pl.BlockSpec(memory_space=pltpu.HBM)
         low, full = jnp.bfloat16, jnp.float32
-        return pl.pallas_call(
+        results = pl.pallas_call(
             functools.partial(kernel, n_section, n_ctx, n_dp),
             out_shape=(
                 jax.ShapeDtypeStruct((1, 1, tokens, width_q), low),
@@ -380,7 +408,7 @@
                 jax.ShapeDtypeStruct((1, width_k), full),
                 jax.ShapeDtypeStruct((1, width_k), full),
             ),
-            in_specs=[anywhere] * 5 + [vmem] * 4,
+            in_specs=[hbm] * 9,
             out_specs=(anywhere, anywhere, anywhere, vmem, vmem, vmem),
             scratch_shapes=[
                 pltpu.VMEM((n_ctx, tokens, GROUP_WIDTH), low),
@@ -410,12 +438,24 @@
                 pltpu.SemaphoreType.DMA((n_ctx, 3)),
                 pltpu.SemaphoreType.DMA((everyone,)),
                 pltpu.SemaphoreType.DMA((everyone,)),
-                pltpu.SemaphoreType.DMA((6,)),
+                pltpu.SemaphoreType.DMA((10,)),
+                pltpu.VMEM(lse.shape, full),
+                pltpu.VMEM(bias_q.shape, low),
+                pltpu.VMEM(key_bias.shape, low),
+                pltpu.VMEM(value_bias.shape, low),
             ],
             compiler_params=pltpu.CompilerParams(
-                collective_id=0, has_side_effects=True, vmem_limit_bytes=40 * 1024 * 1024
+                collective_id=0, has_side_effects=True, vmem_limit_bytes=64 * 1024 * 1024
             ),
         )(q_in, key_in, value_in, out_saved, out_grad, lse, bias_q, key_bias, value_bias)
+        return pl.pallas_call(
+            placing,
+            out_shape=tuple(jax.ShapeDtypeStruct(r.shape, r.dtype) for r in results),
+            in_specs=[anywhere] * 6,
+            out_specs=(hbm,) * 6,
+            scratch_shapes=[pltpu.SemaphoreType.DMA((6,))],
+            compiler_params=pltpu.CompilerParams(vmem_limit_bytes=64 * 1024 * 1024),
+        )(*results)
 
     rows = P("dp", "section", "ctx", None)
     line = P("section", None)

time: 66.8 us -> 81.4 us (1.22)
  Pallas kernels: 54.2 us -> 80.6 us
  local copies, waits for them, and re-layouts: 11.5 us -> 0 us
    pallas_call x0 -> x1, Pallas kernels: none -> 25.4 us  [body(): pl.pallas_call(placing, out_shape=tuple((jax.ShapeDtypeStruct(r.shape, r....]
    unnamed x24 -> x0, local copies, waits for them, and re-layouts: 11.5 us -> none
    pallas_call x1, Pallas kernels: 54.2 us -> 55.2 us  [body(): pl.pallas_call(functools.partial(kernel, n_section, n_ctx, n_dp), out_sha...]
where the time goes in v2:
time: 81.4 us; the launch traced here: 81.2 us
  Pallas kernels  80.6 us (99%)
    pallas_call x1, Pallas kernels, body(): pl.pallas_call(functools.partial(kernel, n_section, n_ctx, n_dp), out_sha...  55.2 us
    pallas_call x1, Pallas kernels, body(): pl.pallas_call(placing, out_shape=tuple((jax.ShapeDtypeStruct(r.shape, r....  25.4 us

profile of v2, /device:TPU:1, one launch (start us, length us, event | category | flops | bytes accessed | tf_op | source)
XLA Modules:
  0.0 81.2 jit_solution(1587777526684813129)
XLA Ops:
  0.6 55.2 %shard_map.136 = (bf16[1,1,128,2048]{3,2,1,0:T(8,128)(2,1)}, bf16[1,1,128,512]{3,2,1,0:T(8,128)(2,1)}, bf16[1,1,128,512]{3,2,1,0:T(8,128)(2,1)}, f32[1,2048]{1,0...) custom-call(bf16[1,1,128,2048]{3,2,1,0:T(8,128)(2,1)} %q_ref.1, bf16[1,1,128,512]{3,2,1,0:T(8,128)(2,1)} %k_ref.1, ...), custom_call_target="tpu_custom_call" | custom-call | tf_op jit(solution)/shard_map/pallas_call | solution.py:401
  55.9 25.4 %shard_map.137 = (bf16[1,1,128,2048]{3,2,1,0:T(8,128)(2,1)}, bf16[1,1,128,512]{3,2,1,0:T(8,128)(2,1)}, bf16[1,1,128,512]{3,2,1,0:T(8,128)(2,1)}, f32[1,2048]{1,0...) custom-call(bf16[1,1,128,2048]{3,2,1,0:T(8,128)(2,1)} %get-tuple-element.12.refs_0_, ...), custom_call_target="tpu_custom_call" | custom-call | tf_op jit(solution)/shard_map/pallas_call | solution.py:451

commit v3 on v2

--- a/solution.py
+++ b/solution.py
@@ -253,7 +253,7 @@
     k_local = lax.broadcasted_iota(jnp.int32, (tokens, 1), 0)
     head_sums = [jnp.zeros((1, HEAD_SIZE), jnp.float32) for _ in range(GROUP)]
 
-    for step in range(n_ctx):
+    for step in [0] + list(reversed(range(1, n_ctx))):
         block = partner(me, step, n_ctx)
         if step:
             for item in (2, 3, 4):
@@ -375,14 +375,21 @@
 
 
 def placing(*refs):
-    sources, targets, sems = refs[:6], refs[6:12], refs[12]
-    copies = [
-        pltpu.make_async_copy(source, target, sems.at[item])
-        for item, (source, target) in enumerate(zip(sources, targets))
+    sources, targets, held, sems = refs[:6], refs[6:12], refs[12:18], refs[18]
+    fetches = [
+        pltpu.make_async_copy(source, slot, sems.at[0, item])
+        for item, (source, slot) in enumerate(zip(sources, held))
     ]
-    for copy in copies:
+    stores = [
+        pltpu.make_async_copy(slot, target, sems.at[1, item])
+        for item, (slot, target) in enumerate(zip(held, targets))
+    ]
+    for copy in fetches:
         copy.start()
-    for copy in copies:
+    for fetch, store in zip(fetches, stores):
+        fetch.wait()
+        store.start()
+    for copy in stores:
         copy.wait()
 
 
@@ -453,7 +460,8 @@
             out_shape=tuple(jax.ShapeDtypeStruct(r.shape, r.dtype) for r in results),
             in_specs=[anywhere] * 6,
             out_specs=(hbm,) * 6,
-            scratch_shapes=[pltpu.SemaphoreType.DMA((6,))],
+            scratch_shapes=[pltpu.VMEM(r.shape, r.dtype) for r in results]
+            + [pltpu.SemaphoreType.DMA((2, 6))],
             compiler_params=pltpu.CompilerParams(vmem_limit_bytes=64 * 1024 * 1024),
         )(*results)
 

time: 81.4 us -> 60.8 us (0.75)
  Pallas kernels: 80.6 us -> 60 us
    pallas_call x1, Pallas kernels: 25.4 us -> 2.02 us  [body(): pl.pallas_call(placing, out_shape=tuple((jax.ShapeDtypeStruct(r.shape, r....]
    pallas_call x1, Pallas kernels: 55.2 us -> 58 us  [body(): pl.pallas_call(functools.partial(kernel, n_section, n_ctx, n_dp), out_sha...]
where the time goes in v3:
time: 60.8 us; the launch traced here: 60.7 us
  Pallas kernels  60 us (99%)
  between operations  0.64 us (1%)
    pallas_call x1, Pallas kernels, body(): pl.pallas_call(functools.partial(kernel, n_section, n_ctx, n_dp), out_sha...  58 us
    pallas_call x1, Pallas kernels, body(): pl.pallas_call(placing, out_shape=tuple((jax.ShapeDtypeStruct(r.shape, r....  2.02 us

profile of v3, /device:TPU:1, one launch (start us, length us, event | category | flops | bytes accessed | tf_op | source)
XLA Modules:
  0.0 60.7 jit_solution(8912641099188699092)
XLA Ops:
  0.6 58.0 %shard_map.136 = (bf16[1,1,128,2048]{3,2,1,0:T(8,128)(2,1)}, bf16[1,1,128,512]{3,2,1,0:T(8,128)(2,1)}, bf16[1,1,128,512]{3,2,1,0:T(8,128)(2,1)}, f32[1,2048]{1,0...) custom-call(bf16[1,1,128,2048]{3,2,1,0:T(8,128)(2,1)} %q_ref.1, bf16[1,1,128,512]{3,2,1,0:T(8,128)(2,1)} %k_ref.1, ...), custom_call_target="tpu_custom_call" | custom-call | tf_op jit(solution)/shard_map/pallas_call | solution.py:408
  58.7 2.0 %shard_map.137 = (bf16[1,1,128,2048]{3,2,1,0:T(8,128)(2,1)}, bf16[1,1,128,512]{3,2,1,0:T(8,128)(2,1)}, bf16[1,1,128,512]{3,2,1,0:T(8,128)(2,1)}, f32[1,2048]{1,0...) custom-call(bf16[1,1,128,2048]{3,2,1,0:T(8,128)(2,1)} %get-tuple-element.12.refs_0_, ...), custom_call_target="tpu_custom_call" | custom-call | tf_op jit(solution)/shard_map/pallas_call | solution.py:458

commit v4 on v3

--- a/solution.py
+++ b/solution.py
@@ -13,6 +13,9 @@
 HEAD_SIZE = 128
 GROUP = QUERY_HEADS // KEY_VALUE_HEADS
 GROUP_WIDTH = GROUP * HEAD_SIZE
+PARTS = 2
+PART_HEADS = GROUP // PARTS
+PART_WIDTH = PART_HEADS * HEAD_SIZE
 MESH = pl.DeviceIdType.MESH
 NT = (((1,), (1,)), ((), ()))
 NN = (((1,), (0,)), ((), ()))
@@ -73,14 +76,16 @@
     out_recv,
     sum_send,
     sum_recv,
+    own_sem,
     local_sem,
     lse_ref,
     bq_ref,
     bk_ref,
     bv_ref,
 ):
-    tokens = q_in.shape[1]
+    tokens = k_in.shape[1]
     half = tokens // 2
+    in_items, out_items = 3 + 2 * PARTS, PARTS + 2
     scale = 1.0 / math.sqrt(HEAD_SIZE)
     section = lax.axis_index("section")
     me = lax.axis_index("ctx")
@@ -105,21 +110,25 @@
     def group_columns(ctx, width):
         return pl.ds(pl.multiple_of(ctx * width, width), width)
 
-    def sources(ctx):
-        wide, narrow = group_columns(ctx, GROUP_WIDTH), group_columns(ctx, HEAD_SIZE)
-        return (
-            (k_ref.at[0, 0, :, narrow], k_in),
-            (v_ref.at[0, 0, :, narrow], v_in),
-            (q_ref.at[0, 0, :, wide], q_in),
-            (g_ref.at[0, 0, :, wide], g_in),
-            (rows_out.at[ctx], rows_in),
-        )
+    def transfer(item, ctx, slot):
+        narrow = group_columns(ctx, HEAD_SIZE)
+        if item == 0:
+            return k_ref.at[0, 0, :, narrow], k_in.at[slot]
+        if item == 1:
+            return v_ref.at[0, 0, :, narrow], v_in.at[slot]
+        if item == 2:
+            return rows_out.at[ctx], rows_in.at[slot]
+        part = (item - 3) // 2
+        wide = group_columns(ctx * PARTS + part, PART_WIDTH)
+        if item % 2:
+            return q_ref.at[0, 0, :, wide], q_in.at[slot, part]
+        return g_ref.at[0, 0, :, wide], g_in.at[slot, part]
 
     def in_copy(item, to, slot):
-        source, target = sources(to)[item]
+        source, target = transfer(item, to, slot)
         return pltpu.make_async_remote_copy(
             src_ref=source,
-            dst_ref=target.at[slot],
+            dst_ref=target,
             send_sem=in_send.at[to, item],
             recv_sem=in_recv.at[slot, item],
             device_id=ctx_device(to),
@@ -127,28 +136,26 @@
         )
 
     def own_copy(item):
-        source, target = sources(me)[item]
-        return pltpu.make_async_copy(source, target.at[me], local_sem.at[item])
-
-    def out_copies(ctx, slot):
-        wide, narrow = group_columns(slot, GROUP_WIDTH), group_columns(slot, HEAD_SIZE)
-        return [
-            pltpu.make_async_remote_copy(
-                src_ref=source.at[ctx],
-                dst_ref=target,
-                send_sem=out_send.at[ctx, item],
-                recv_sem=out_recv.at[slot, item],
-                device_id=before_device(ctx),
-                device_id_type=MESH,
-            )
-            for item, (source, target) in enumerate(
-                (
-                    (q_out, rq_ref.at[0, 0, :, wide]),
-                    (k_out, rk_ref.at[0, 0, :, narrow]),
-                    (v_out, rv_ref.at[0, 0, :, narrow]),
-                )
-            )
-        ]
+        source, target = transfer(item, me, me)
+        return pltpu.make_async_copy(source, target, own_sem.at[item])
+
+    def out_copy(item, ctx, slot):
+        narrow = group_columns(slot, HEAD_SIZE)
+        if item < PARTS:
+            wide = group_columns(slot * PARTS + item, PART_WIDTH)
+            source, target = q_out.at[ctx, item], rq_ref.at[0, 0, :, wide]
+        elif item == PARTS:
+            source, target = k_out.at[ctx], rk_ref.at[0, 0, :, narrow]
+        else:
+            source, target = v_out.at[ctx], rv_ref.at[0, 0, :, narrow]
+        return pltpu.make_async_remote_copy(
+            src_ref=source,
+            dst_ref=target,
+            send_sem=out_send.at[ctx, item],
+            recv_sem=out_recv.at[slot, item],
+            device_id=before_device(ctx),
+            device_id_type=MESH,
+        )
 
     def sum_copy(place, slot):
         return pltpu.make_async_remote_copy(
@@ -193,17 +200,21 @@
     g_copy.start()
     for copy in small_copies:
         copy.start()
-    for item in range(4):
+    own_items = [item for item in range(in_items) if item != 2]
+    for item in own_items:
         own_copy(item).start()
     bias[:, :GROUP_WIDTH] = jnp.zeros((8, GROUP_WIDTH), jnp.float32)
 
     neighbours = jnp.where(has_before, n_ctx, 0) + jnp.where(has_after, n_ctx, 0)
     pl.semaphore_wait(barrier, everyone - 1 + neighbours)
 
-    for items in ((0, 1), (2, 3)):
+    def send(items):
         for step in reversed(range(1, n_ctx)):
             for item in items:
                 in_copy(item, partner(me, step, n_ctx), me).start()
+
+    send((0, 1))
+    send((3, 4))
 
     o_copy.wait()
     g_copy.wait()
@@ -216,8 +227,9 @@
             product = g_own[:, columns].astype(jnp.float32) * o_own[:, columns].astype(jnp.float32)
             lines.append(jnp.sum(product.T, axis=0, keepdims=True))
         rows_out[group] = jnp.concatenate(lines, axis=0)
-    for step in reversed(range(1, n_ctx)):
-        in_copy(4, partner(me, step, n_ctx), me).start()
+    send((2,))
+    for part in range(1, PARTS):
+        send((3 + 2 * part, 4 + 2 * part))
     rows_in[me] = rows_out[me]
 
     for ctx in range(n_ctx):
@@ -230,7 +242,7 @@
             bias[1:2, :HEAD_SIZE] = bk_ref[:, narrow].astype(jnp.float32)
             bias[2:3, :HEAD_SIZE] = bv_ref[:, narrow].astype(jnp.float32)
 
-    for item in range(4):
+    for item in own_items:
         own_copy(item).wait()
     for step in range(1, n_ctx):
         for item in (0, 1):
@@ -248,27 +260,33 @@
         return jnp.where(local < half, block * half + local, late)
 
     q_local = jnp.concatenate(
-        [lax.broadcasted_iota(jnp.int32, (1, tokens), 1)] * GROUP, axis=1
+        [lax.broadcasted_iota(jnp.int32, (1, tokens), 1)] * PART_HEADS, axis=1
     )
     k_local = lax.broadcasted_iota(jnp.int32, (tokens, 1), 0)
     head_sums = [jnp.zeros((1, HEAD_SIZE), jnp.float32) for _ in range(GROUP)]
 
-    for step in [0] + list(reversed(range(1, n_ctx))):
+    order = [(part, 0) for part in range(PARTS)]
+    order += [(part, step) for part in range(PARTS) for step in range(1, n_ctx)]
+    for part, step in order:
         block = partner(me, step, n_ctx)
         if step:
-            for item in (2, 3, 4):
+            for item in ((2,) if part == 0 else ()) + (3 + 2 * part, 4 + 2 * part):
                 in_copy(item, block, block).wait_recv()
-        for head in range(GROUP):
+        for head in range(PART_HEADS):
             columns = slice(head * HEAD_SIZE, (head + 1) * HEAD_SIZE)
+            wide = slice(
+                part * PART_WIDTH + head * HEAD_SIZE, part * PART_WIDTH + (head + 1) * HEAD_SIZE
+            )
             rows = slice(head * tokens, (head + 1) * tokens)
             q_stack[rows] = (
-                q_in[block, :, columns].astype(jnp.float32) + bias[0:1, columns]
+                q_in[block, part, :, columns].astype(jnp.float32) + bias[0:1, wide]
             ).astype(jnp.bfloat16)
-            g_stack[rows] = g_in[block, :, columns]
+            g_stack[rows] = g_in[block, part, :, columns]
         grad_q_turned[...] = jnp.zeros_like(grad_q_turned)
         lines = rows_in[block]
-        lse_line = jnp.concatenate([lines[h : h + 1] for h in range(GROUP)], axis=1)
-        delta_line = jnp.concatenate([lines[GROUP + h : GROUP + h + 1] for h in range(GROUP)], axis=1)
+        heads = range(part * PART_HEADS, (part + 1) * PART_HEADS)
+        lse_line = jnp.concatenate([lines[h : h + 1] for h in heads], axis=1)
+        delta_line = jnp.concatenate([lines[GROUP + h : GROUP + h + 1] for h in heads], axis=1)
         q_pos = positions(block, q_local)
 
         def over_keys(owner, _):
@@ -295,14 +313,15 @@
             return 0
 
         lax.fori_loop(0, n_ctx, over_keys, 0)
-        for head in range(GROUP):
+        for head in range(PART_HEADS):
+            columns = slice(head * HEAD_SIZE, (head + 1) * HEAD_SIZE)
             grad_q = grad_q_turned[:, head * tokens : (head + 1) * tokens].T * scale
-            head_sums[head] += jnp.sum(grad_q, axis=0, keepdims=True)
-            q_out[block, :, head * HEAD_SIZE : (head + 1) * HEAD_SIZE] = grad_q.astype(jnp.bfloat16)
+            head_sums[part * PART_HEADS + head] += jnp.sum(grad_q, axis=0, keepdims=True)
+            q_out[block, part, :, columns] = grad_q.astype(jnp.bfloat16)
 
         @pl.when(has_before)
         def _():
-            out_copies(block, me)[0].start()
+            out_copy(part, block, me).start()
 
     key_sum = jnp.zeros((1, HEAD_SIZE), jnp.float32)
     value_sum = jnp.zeros((1, HEAD_SIZE), jnp.float32)
@@ -321,8 +340,8 @@
     @pl.when(has_before)
     def _():
         for step in reversed(range(n_ctx)):
-            for copy in out_copies(partner(me, step, n_ctx), me)[1:]:
-                copy.start()
+            for item in range(PARTS, out_items):
+                out_copy(item, partner(me, step, n_ctx), me).start()
 
     @pl.when(section == n_section - 1)
     def _():
@@ -356,7 +375,7 @@
         sum_v_ref[:, narrow] = total[GROUP + 1 : GROUP + 2]
 
     for step in range(1, n_ctx):
-        for item in range(5):
+        for item in range(in_items):
             in_copy(item, partner(me, step, n_ctx), me).wait_send()
     for step in range(1, everyone):
         sum_copy((my_place + step) % everyone, my_place).wait_send()
@@ -364,14 +383,14 @@
     @pl.when(has_before)
     def _():
         for ctx in range(n_ctx):
-            for copy in out_copies(ctx, me):
-                copy.wait_send()
+            for item in range(out_items):
+                out_copy(item, ctx, me).wait_send()
 
     @pl.when(has_after)
     def _():
         for ctx in range(n_ctx):
-            for copy in out_copies(ctx, ctx):
-                copy.wait_recv()
+            for item in range(out_items):
+                out_copy(item, ctx, ctx).wait_recv()
 
 
 def placing(*refs):
@@ -418,8 +437,8 @@
             in_specs=[hbm] * 9,
             out_specs=(anywhere, anywhere, anywhere, vmem, vmem, vmem),
             scratch_shapes=[
-                pltpu.VMEM((n_ctx, tokens, GROUP_WIDTH), low),
-                pltpu.VMEM((n_ctx, tokens, GROUP_WIDTH), low),
+                pltpu.VMEM((n_ctx, PARTS, tokens, PART_WIDTH), low),
+                pltpu.VMEM((n_ctx, PARTS, tokens, PART_WIDTH), low),
                 pltpu.VMEM((n_ctx, tokens, HEAD_SIZE), low),
                 pltpu.VMEM((n_ctx, tokens, HEAD_SIZE), low),
                 pltpu.VMEM((n_ctx, 2 * GROUP, tokens), full),
@@ -432,19 +451,20 @@
                 pltpu.VMEM((n_ctx, HEAD_SIZE, tokens), low),
                 pltpu.VMEM((n_ctx, tokens, HEAD_SIZE), full),
                 pltpu.VMEM((n_ctx, tokens, HEAD_SIZE), full),
-                pltpu.VMEM((HEAD_SIZE, GROUP * tokens), full),
-                pltpu.VMEM((GROUP * tokens, HEAD_SIZE), low),
-                pltpu.VMEM((GROUP * tokens, HEAD_SIZE), low),
-                pltpu.VMEM((n_ctx, tokens, GROUP_WIDTH), low),
+                pltpu.VMEM((HEAD_SIZE, PART_HEADS * tokens), full),
+                pltpu.VMEM((PART_HEADS * tokens, HEAD_SIZE), low),
+                pltpu.VMEM((PART_HEADS * tokens, HEAD_SIZE), low),
+                pltpu.VMEM((n_ctx, PARTS, tokens, PART_WIDTH), low),
                 pltpu.VMEM((n_ctx, tokens, HEAD_SIZE), low),
                 pltpu.VMEM((n_ctx, tokens, HEAD_SIZE), low),
                 pltpu.VMEM((everyone, 8, HEAD_SIZE), full),
-                pltpu.SemaphoreType.DMA((n_ctx, 5)),
-                pltpu.SemaphoreType.DMA((n_ctx, 5)),
-                pltpu.SemaphoreType.DMA((n_ctx, 3)),
-                pltpu.SemaphoreType.DMA((n_ctx, 3)),
+                pltpu.SemaphoreType.DMA((n_ctx, 3 + 2 * PARTS)),
+                pltpu.SemaphoreType.DMA((n_ctx, 3 + 2 * PARTS)),
+                pltpu.SemaphoreType.DMA((n_ctx, PARTS + 2)),
+                pltpu.SemaphoreType.DMA((n_ctx, PARTS + 2)),
                 pltpu.SemaphoreType.DMA((everyone,)),
                 pltpu.SemaphoreType.DMA((everyone,)),
+                pltpu.SemaphoreType.DMA((3 + 2 * PARTS,)),
                 pltpu.SemaphoreType.DMA((10,)),
                 pltpu.VMEM(lse.shape, full),
                 pltpu.VMEM(bias_q.shape, low),

time: 60.8 us -> 58.2 us (0.957)
  Pallas kernels: 60 us -> 57.4 us
    pallas_call x1, Pallas kernels: 58 us -> 55.4 us  [body(): pl.pallas_call(functools.partial(kernel, n_section, n_ctx, n_dp), out_sha...]
where the time goes in v4:
time: 58.2 us; the launch traced here: 58.1 us
  Pallas kernels  57.4 us (99%)
  between operations  0.64 us (1%)
    pallas_call x1, Pallas kernels, body(): pl.pallas_call(functools.partial(kernel, n_section, n_ctx, n_dp), out_sha...  55.4 us
    pallas_call x1, Pallas kernels, body(): pl.pallas_call(placing, out_shape=tuple((jax.ShapeDtypeStruct(r.shape, r....  2.02 us

profile of v4, /device:TPU:1, one launch (start us, length us, event | category | flops | bytes accessed | tf_op | source)
XLA Modules:
  0.0 58.1 jit_solution(5987423651813745782)
XLA Ops:
  0.6 55.4 %shard_map.136 = (bf16[1,1,128,2048]{3,2,1,0:T(8,128)(2,1)}, bf16[1,1,128,512]{3,2,1,0:T(8,128)(2,1)}, bf16[1,1,128,512]{3,2,1,0:T(8,128)(2,1)}, f32[1,2048]{1,0...) custom-call(bf16[1,1,128,2048]{3,2,1,0:T(8,128)(2,1)} %q_ref.1, bf16[1,1,128,512]{3,2,1,0:T(8,128)(2,1)} %k_ref.1, ...), custom_call_target="tpu_custom_call" | custom-call | tf_op jit(solution)/shard_map/pallas_call | solution.py:427
  56.0 2.0 %shard_map.137 = (bf16[1,1,128,2048]{3,2,1,0:T(8,128)(2,1)}, bf16[1,1,128,512]{3,2,1,0:T(8,128)(2,1)}, bf16[1,1,128,512]{3,2,1,0:T(8,128)(2,1)}, f32[1,2048]{1,0...) custom-call(bf16[1,1,128,2048]{3,2,1,0:T(8,128)(2,1)} %get-tuple-element.12.refs_0_, ...), custom_call_target="tpu_custom_call" | custom-call | tf_op jit(solution)/shard_map/pallas_call | solution.py:478
